TPU v7x, 32 devices: a whole 2x2x4 slice. The times are simulated.
32 devices in a mesh: groups: 2 (over x), blk: 16 (over z, y, core).
Axes of the slice: x: 2, y: 2, z: 4, core: 2. Of those that a mesh axis runs over, the one named last changes fastest.
Arguments:
- frames: bfloat16 [256, 16384], P(('groups', 'blk')), parts along dimension 0
- basis: bfloat16 [256, 64], P(('groups', 'blk')), parts along dimension 0, may hold values from -6 to 6
- density: bfloat16 [256], P(('groups', 'blk')), parts along dimension 0, may hold values from 0.25 to 4
Outputs:
- residual_block: bfloat16 [256, 64], P(('groups', 'blk')), parts along dimension 0
- coefficients: float32 [128, 64], P('groups'), parts along dimension 0
There are 2 independent parts, one for each index of `groups`. A program takes and returns all parts, laid end to end along the dimension named above; each array names one. Nothing has to cross between parts.
All inputs are finite; a program needn't handle non-finite values.
Results may differ from a plain program's by a relative error of at most 0.0045.
Values may be sent and summed in bfloat16 or wider, within the bound.
A program may use at most 64 MiB of HBM per device.

v0:
```python
import jax
import jax.numpy as jnp
from jax import lax
from jax.sharding import PartitionSpec as P


def pair_kernel(left, left_norms, right):
    right_norms = jnp.sum(jnp.square(right.astype(jnp.float32)), axis=1)
    inner_products = lax.dot_general(
        left, right, (((1,), (1,)), ((), ())), preferred_element_type=jnp.float32
    )
    squared_dist = left_norms[:, None] + right_norms[None, :] - 2.0 * inner_products
    return jnp.exp(-squared_dist / left.shape[1])


def shards(frames, basis, density):
    own_norms = jnp.sum(jnp.square(frames.astype(jnp.float32)), axis=1)
    row_count = frames.shape[0]
    blocks = lax.all_gather(frames, "blk", axis=0, tiled=True)
    vectors = lax.all_gather(basis, "blk", axis=0, tiled=True)
    weights_in = lax.all_gather(density, "blk", axis=0, tiled=True)
    kernel = pair_kernel(frames, own_norms, blocks)
    forward = (kernel * weights_in.astype(jnp.float32)[None, :]).astype(jnp.bfloat16)
    numer = jnp.dot(forward, vectors, preferred_element_type=jnp.float32)
    totals = jnp.sum(forward.astype(jnp.float32), axis=1)
    numer, totals = (numer, totals)
    applied = numer / totals[:, None]
    basis_f = basis.astype(jnp.float32)
    local_coef = lax.dot_general(
        basis_f,
        applied,
        (((0,), (0,)), ((), ())),
        precision=lax.Precision.HIGHEST,
        preferred_element_type=jnp.float32,
    )
    coefficients = lax.psum(local_coef, "blk")
    frame_total = row_count * lax.axis_size("blk")
    projection = jnp.dot(
        basis_f, coefficients, precision=lax.Precision.HIGHEST, preferred_element_type=jnp.float32
    )
    residual_block = (applied - projection / frame_total).astype(jnp.bfloat16)
    return (residual_block, coefficients)


def solution(mesh):
    placed = (P(("groups", "blk"), None), P(("groups", "blk"), None), P(("groups", "blk")))
    return jax.shard_map(
        shards,
        mesh=mesh,
        in_specs=placed,
        out_specs=(P(("groups", "blk"), None), P("groups", None)),
        check_vma=False,
    )
```

profile of v0, /device:TPU:0, one launch (start us, length us, event | category | flops | bytes accessed | tf_op | source)
XLA Modules:
  0.0 137.7 jit_solution(3754534518135585667)
XLA Ops:
  7.2 0.0 copy-start.1
  7.2 0.0 all-gather.2.cloned.1.call-start
  7.2 0.7 all-gather.2.cloned.1.call-update
  7.9 1.2 dynamic-slice
  9.8 0.9 dynamic-update-slice
  10.7 35.4 %all-reduce = bf16[128]{0:T(256)(128)(2,1)S(1)} all-reduce(bf16[128]{0:T(256)(128)(2,1)S(1)} %dynamic-update-slice), channel_id=1, replica_groups=mesh['groups'=2,'blk'=16] {'blk'}, use_global_device_ids=true, to_apply=%add | all-reduce | flops 128 | bytes 512
  46.1 17.6 %all_gather.11 = bf16[128,64]{1,0:T(8,128)(2,1)S(1)} all-gather(bf16[8,64]{1,0:T(8,128)(2,1)} %param.4), channel_id=1, replica_groups=mesh['groups'=2,'blk'=16] {'blk'}, dimensions={0}, use_global_device_ids=true | all-gather | bytes 17408 | tf_op jit(solution)/shard_map/all_gather | solution.py:20
  63.7 1.2 multiply_reduce_fusion.1
  64.9 0.0 all-gather.2.cloned.1.call-done
  64.9 0.0 copy-start
  64.9 0.0 copy-start.2
  64.9 3.2 %multiply_reduce_fusion = f32[128]{0:T(128)S(1)} fusion(bf16[128,16384]{1,0:T(8,128)(2,1)} %all-gather.2.cloned.1.call-done), kind=kLoop, calls=%fused_computation | loop fusion | flops 6291328 | bytes 4194816 | tf_op jit(solution)/shard_map/reduce_sum | solution.py:8
  68.2 0.0 copy-done.1
  68.2 0.2 copy-done
  68.4 1.3 convert_reduce_fusion
  69.7 0.1 convolution_divide_fusion
  69.8 0.0 copy-done.2
  69.8 0.2 convolution_bitcast_fusion
  70.0 59.3 %psum.7 = f32[64,64]{0,1:T(8,128)S(1)} all-reduce(f32[64,64]{0,1:T(8,128)S(1)} %convolution_bitcast_fusion), channel_id=1, replica_groups=mesh['groups'=2,'blk'=16] {'blk'}, use_global_device_ids=true, to_apply=%region_3.0 | all-reduce | flops 4096 | bytes 32768 | tf_op jit(solution)/shard_map/psum | solution.py:36
  129.4 0.7 fusion.8
  130.1 0.7 copy.5
  (2 shorter events, 0.0 us)
Async XLA Ops:
  7.2 61.0 %copy-start.1 = (bf16[8,16384]{1,0:T(8,128)(2,1)S(1)}, bf16[8,16384]{1,0:T(8,128)(2,1)}, u32[]{:S(2)}) copy-start(bf16[8,16384]{1,0:T(8,128)(2,1)} %param.3) | copy-start | bytes 786436
  7.2 57.7 %all-gather.2.cloned.1.call-start = ((), (), s32[]{:S(2)}) async-start(), calls=%async_computation | async-start | bytes 4456448 | tf_op jit(solution)/shard_map/all_gather | solution.py:19
  64.9 3.5 %copy-start = (bf16[128,16384]{1,0:T(8,128)(2,1)S(1)}, bf16[128,16384]{1,0:T(8,128)(2,1)}, u32[]{:S(2)}) copy-start(bf16[128,16384]{1,0:T(8,128)(2,1)} %all-gather.2.cloned.1.call-done) | copy-start | bytes 12582916
  64.9 4.9 %copy-start.2 = (bf16[8,64]{1,0:T(8,128)(2,1)S(1)}, bf16[8,64]{1,0:T(8,128)(2,1)}, u32[]{:S(2)}) copy-start(bf16[8,64]{1,0:T(8,128)(2,1)} %param.4) | copy-start | bytes 3076
Sparse Core Ops, SparseCore 0:
  10.2 53.5 all-gather.1
where the time goes:
time: 138 us
  blocking collectives  112 us (81%)
  between operations  14.7 us (11%)
  other arithmetic  4.43 us (3%)
  local copies, waits for them, and re-layouts  3.01 us (2%)
  matrix products  2.4 us (2%)
    psum x1, blocking collectives, shards(): coefficients = lax.psum(local_coef, 'blk')  59.3 us
    unnamed x1, blocking collectives  35.4 us
    all_gather x1, blocking collectives, shards(): vectors = lax.all_gather(basis, 'blk', axis=0, tiled=True)  17.6 us
    reduce_sum x1, other arithmetic, pair_kernel(): right_norms = jnp.sum(jnp.square(right.astype(jnp.float32)), axis=1)  3.23 us
    unnamed x10, local copies, waits for them, and re-layouts  3.01 us
  transfers between devices with their start and end apart: 1, of which 0 were waited for; matrix products, arithmetic and copies ran while one was open for 2% of the time, Pallas kernels for 0%

commit v1 on v0

v1 whole, which is shorter than its diff:
```python
import functools

import jax
import jax.numpy as jnp
from jax import lax
from jax.experimental import pallas as pl
from jax.experimental.pallas import tpu as pltpu
from jax.sharding import PartitionSpec as P

LANES = 128


def partners(me, n):
    half = n // 2
    mine = me // half
    far = [(1 - mine) * half + lax.rem(me + j, half) for j in range(half)]
    near = [mine * half + lax.rem(me + j, half) for j in range(1, half)]
    return far + near


def kernel(
    n,
    frames_ref,
    basis_ref,
    density_ref,
    residual_ref,
    coef_ref,
    gathered,
    aux,
    partial,
    arrived,
    applied,
    own_sem,
    send_sem,
    recv_sem,
):
    me = lax.axis_index("blk")
    rows, features = frames_ref.shape
    width = basis_ref.shape[1]
    span = features // n
    total = n * rows
    others = partners(me, n)

    barrier = pltpu.get_barrier_semaphore()
    for other in others:
        pl.semaphore_signal(
            barrier, inc=1, device_id={"blk": other}, device_id_type=pl.DeviceIdType.MESH
        )

    own = pltpu.make_async_copy(
        frames_ref.at[:, pl.ds(pl.multiple_of(me * span, span), span)], gathered.at[me], own_sem
    )
    own.start()

    row_id = lax.broadcasted_iota(jnp.int32, (rows, rows), 0)
    col_id = lax.broadcasted_iota(jnp.int32, (rows, rows), 1)
    density_row = density_ref[...].astype(jnp.float32)
    density_col = jnp.sum(
        jnp.where(row_id == col_id, jnp.broadcast_to(density_row, (rows, rows)), 0.0),
        axis=1,
        keepdims=True,
    )
    own_basis = basis_ref[...].astype(jnp.float32)
    own_wide = jnp.concatenate(
        [own_basis, jnp.broadcast_to(density_col, (rows, LANES - width))], axis=1
    )
    aux[me] = own_wide.astype(jnp.bfloat16)

    pl.semaphore_wait(barrier, n - 1)

    def send(src, dst, slot, other):
        pltpu.make_async_remote_copy(
            src_ref=src,
            dst_ref=dst,
            send_sem=send_sem.at[slot],
            recv_sem=recv_sem.at[slot],
            device_id={"blk": other},
            device_id_type=pl.DeviceIdType.MESH,
        ).start()

    def wait_all(buffer, sem):
        part = buffer.at[pl.ds(0, n - 1)]
        pltpu.make_async_copy(part, part, sem).wait()

    for other in others:
        send(
            frames_ref.at[:, pl.ds(pl.multiple_of(other * span, span), span)],
            gathered.at[me],
            0,
            other,
        )
    for other in others:
        send(aux.at[me], aux.at[me], 1, other)

    wait_all(aux, recv_sem.at[1])
    wide = aux[...].astype(jnp.float32).reshape(total, LANES)
    eye = lax.broadcasted_iota(jnp.int32, (total, total), 0) == lax.broadcasted_iota(
        jnp.int32, (total, total), 1
    )
    density_all = jnp.sum(jnp.where(eye, wide[:, width : width + 1], 0.0), axis=0, keepdims=True)
    lane = lax.broadcasted_iota(jnp.int32, (total, LANES), 1)
    vectors = jnp.where(lane < width, wide, 0.0)
    vectors_bf = vectors.astype(jnp.bfloat16)
    own_lane = lax.broadcasted_iota(jnp.int32, (rows, LANES), 1)
    own_vectors = jnp.where(own_lane < width, own_wide, 0.0)
    overlap = lax.dot_general(
        own_vectors.astype(jnp.bfloat16),
        vectors_bf,
        (((1,), (1,)), ((), ())),
        preferred_element_type=jnp.float32,
    )
    onto = jnp.concatenate([jnp.transpose(vectors)[:width], overlap], axis=0)

    own.wait()
    wait_all(gathered, recv_sem.at[0])
    block = gathered[...].reshape(total, span)
    gram = lax.dot_general(
        block, block, (((1,), (1,)), ((), ())), preferred_element_type=jnp.float32
    )
    diagonal = jnp.where(eye, gram, 0.0)
    dist = (
        jnp.sum(diagonal, axis=1, keepdims=True)
        + jnp.sum(diagonal, axis=0, keepdims=True)
        - 2.0 * gram
    )
    partial[...] = dist.reshape(n, rows, total)
    for other in others:
        send(partial.at[other], arrived.at[me], 2, other)
    arrived[me] = partial[me]
    wait_all(arrived, recv_sem.at[2])

    squared_dist = jnp.sum(arrived[...], axis=0)
    weight = (jnp.exp(-squared_dist / features) * density_all).astype(jnp.bfloat16)
    numer = jnp.dot(weight, vectors_bf, preferred_element_type=jnp.float32)
    totals = jnp.sum(weight.astype(jnp.float32), axis=1, keepdims=True)
    own_applied = numer / totals
    applied[me] = own_applied
    for other in others:
        send(applied.at[me], applied.at[me], 3, other)
    wait_all(applied, recv_sem.at[3])

    products = jnp.dot(
        onto,
        applied[...].reshape(total, LANES),
        precision=lax.Precision.HIGHEST,
        preferred_element_type=jnp.float32,
    )
    coef_ref[...] = products[:width, :width]
    residual = own_applied - products[width:] / total
    residual_ref[...] = residual[:, :width].astype(jnp.bfloat16)

    wait_all(gathered, send_sem.at[0])
    wait_all(aux, send_sem.at[1])
    wait_all(arrived, send_sem.at[2])
    wait_all(applied, send_sem.at[3])


def shards(n, frames, basis, density):
    rows, features = frames.shape
    width = basis.shape[1]
    total = n * rows
    vmem = pl.BlockSpec(memory_space=pltpu.VMEM)
    return pl.pallas_call(
        functools.partial(kernel, n),
        out_shape=(
            jax.ShapeDtypeStruct((rows, width), jnp.bfloat16),
            jax.ShapeDtypeStruct((width, width), jnp.float32),
        ),
        in_specs=[pl.BlockSpec(memory_space=pl.ANY), vmem, vmem],
        out_specs=(vmem, vmem),
        scratch_shapes=[
            pltpu.VMEM((n, rows, features // n), jnp.bfloat16),
            pltpu.VMEM((n, rows, LANES), jnp.bfloat16),
            pltpu.VMEM((n, rows, total), jnp.float32),
            pltpu.VMEM((n, rows, total), jnp.float32),
            pltpu.VMEM((n, rows, LANES), jnp.float32),
            pltpu.SemaphoreType.DMA,
            pltpu.SemaphoreType.DMA((4,)),
            pltpu.SemaphoreType.DMA((4,)),
        ],
        compiler_params=pltpu.CompilerParams(
            collective_id=0, has_side_effects=True, vmem_limit_bytes=32 * 1024 * 1024
        ),
        cost_estimate=pl.CostEstimate(
            flops=2 * total * total * (features // n),
            bytes_accessed=2 * rows * features,
            transcendentals=rows * total,
        ),
    )(frames, basis, density.reshape(1, rows))


def solution(mesh):
    placed = (P(("groups", "blk"), None), P(("groups", "blk"), None), P(("groups", "blk")))
    return jax.shard_map(
        functools.partial(shards, mesh.shape["blk"]),
        mesh=mesh,
        in_specs=placed,
        out_specs=(P(("groups", "blk"), None), P("groups", None)),
        check_vma=False,
    )
```

time: 138 us -> 27.3 us (0.20)
  blocking collectives: 112 us -> 0 us
  Pallas kernels: 0 us -> 23 us
  between operations: 14.7 us -> 0.65 us
  other arithmetic: 4.43 us -> 0 us
  matrix products: 2.4 us -> 0 us
    psum x1 -> x0, blocking collectives: 59.3 us -> none  [shards(): coefficients = lax.psum(local_coef, 'blk')]
    unnamed x1 -> x0, blocking collectives: 35.4 us -> none
    pallas_call x0 -> x1, Pallas kernels: none -> 23 us  [shards(): pl.pallas_call(functools.partial(kernel, n), out_shape=(jax.ShapeDtypeStr...]
    all_gather x1 -> x0, blocking collectives: 17.6 us -> none  [shards(): vectors = lax.all_gather(basis, 'blk', axis=0, tiled=True)]
    reduce_sum x2 -> x0, other arithmetic: 4.43 us -> none  [the longest x1 3.23 us: pair_kernel(): right_norms = jnp.sum(jnp.square(right.astype(jnp.float32)), axis=1)]
    dot_general x4 -> x0, matrix products: 2.4 us -> none  [the longest x1 1.3 us: pair_kernel(): lax.dot_general(left, right, (((1,), (1,)), ((), ())), preferred_element_...]
    unnamed x10 -> x8, local copies, waits for them, and re-layouts: 3.01 us -> 3.47 us
  transfers between devices with their start and end apart: 1 -> 0, of which waited for: 0 -> 0; matrix products, arithmetic and copies ran while one was open for 2% -> 0% of each run, Pallas kernels for 0% -> 0%
where the time goes in v1:
time: 27.3 us; the launch traced here: 27.2 us
  Pallas kernels  23 us (84%)
  local copies, waits for them, and re-layouts  3.47 us (13%)
  between operations  0.65 us (2%)
    pallas_call x1, Pallas kernels, shards(): pl.pallas_call(functools.partial(kernel, n), out_shape=(jax.ShapeDtypeStr...  23 us
    unnamed x8, local copies, waits for them, and re-layouts  3.47 us

profile of v1, /device:TPU:0, one launch (start us, length us, event | category | flops | bytes accessed | tf_op | source)
XLA Modules:
  0.0 27.2 jit_solution(6252152141459826152)
XLA Ops:
  0.6 0.0 copy-start.2
  0.6 0.6 %copy-done.2 = bf16[8]{0:T(256)(128)(2,1)S(1)} copy-done((bf16[8]{0:T(256)(128)(2,1)S(1)}, bf16[8]{0:T(256)(128)(2,1)}, u32[]{:S(2)}) %copy-start.2) | copy-done | bytes 40
  1.3 0.0 copy-start
  1.3 0.9 %copy-done = bf16[8,16384]{1,0:T(8,128)(2,1)S(1)} copy-done((bf16[8,16384]{1,0:T(8,128)(2,1)S(1)}, bf16[8,16384]{1,0:T(8,128)(2,1)}, u32[]{:S(2)}) %copy-start) | copy-done | bytes 262168
  2.2 0.0 copy-start.1
  2.2 0.7 %copy-done.1 = bf16[8,64]{1,0:T(8,128)(2,1)S(1)} copy-done((bf16[8,64]{1,0:T(8,128)(2,1)S(1)}, bf16[8,64]{1,0:T(8,128)(2,1)}, u32[]{:S(2)}) %copy-start.1) | copy-done | bytes 1048
  2.9 23.0 %shard_map.50 = (bf16[8,64]{1,0:T(8,128)(2,1)S(1)}, f32[64,64]{1,0:T(8,128)S(1)}) custom-call(bf16[8,16384]{1,0:T(8,128)(2,1)S(1)} %copy-done, bf16[8,64]{1,0:T(8,128)(2,1)S(1)} %copy-done.1, bf16[1,8]{1,0:T(2,128)(2,1)S(1)} %bitcast.1), custom_call_target="tpu_custom_call" | custom-call | flops 33554432 | bytes 262144 | tf_op jit(solution)/shard_map/pallas_call | solution.py:163
  26.0 0.6 %copy.7 = bf16[8,64]{1,0:T(8,128)(2,1)} copy(bf16[8,64]{1,0:T(8,128)(2,1)S(1)} %get-tuple-element.4) | data formatting | bytes 2048
  26.5 0.6 %copy.8 = f32[64,64]{1,0:T(8,128)} copy(f32[64,64]{1,0:T(8,128)S(1)} %get-tuple-element.5) | data formatting | bytes 32768
Async XLA Ops:
  0.6 0.7 %copy-start.2 = (bf16[8]{0:T(256)(128)(2,1)S(1)}, bf16[8]{0:T(256)(128)(2,1)}, u32[]{:S(2)}) copy-start(bf16[8]{0:T(256)(128)(2,1)} %param.5) | copy-start | bytes 52
  1.3 0.9 %copy-start = (bf16[8,16384]{1,0:T(8,128)(2,1)S(1)}, bf16[8,16384]{1,0:T(8,128)(2,1)}, u32[]{:S(2)}) copy-start(bf16[8,16384]{1,0:T(8,128)(2,1)} %frames_ref.1) | copy-start | bytes 786436
  2.2 0.7 %copy-start.1 = (bf16[8,64]{1,0:T(8,128)(2,1)S(1)}, bf16[8,64]{1,0:T(8,128)(2,1)}, u32[]{:S(2)}) copy-start(bf16[8,64]{1,0:T(8,128)(2,1)} %basis_ref.1) | copy-start | bytes 3076

commit v2 on v1

--- a/solution.py
+++ b/solution.py
@@ -30,6 +30,8 @@
     partial,
     arrived,
     applied,
+    basis_vmem,
+    density_vmem,
     own_sem,
     send_sem,
     recv_sem,
@@ -41,6 +43,11 @@
     total = n * rows
     others = partners(me, n)
 
+    fetch_basis = pltpu.make_async_copy(basis_ref, basis_vmem, own_sem.at[1])
+    fetch_basis.start()
+    fetch_density = pltpu.make_async_copy(density_ref, density_vmem, own_sem.at[2])
+    fetch_density.start()
+
     barrier = pltpu.get_barrier_semaphore()
     for other in others:
         pl.semaphore_signal(
@@ -48,19 +55,21 @@
         )
 
     own = pltpu.make_async_copy(
-        frames_ref.at[:, pl.ds(pl.multiple_of(me * span, span), span)], gathered.at[me], own_sem
+        frames_ref.at[:, pl.ds(pl.multiple_of(me * span, span), span)], gathered.at[me], own_sem.at[0]
     )
     own.start()
 
     row_id = lax.broadcasted_iota(jnp.int32, (rows, rows), 0)
     col_id = lax.broadcasted_iota(jnp.int32, (rows, rows), 1)
-    density_row = density_ref[...].astype(jnp.float32)
+    fetch_density.wait()
+    density_row = density_vmem[...].astype(jnp.float32)
     density_col = jnp.sum(
         jnp.where(row_id == col_id, jnp.broadcast_to(density_row, (rows, rows)), 0.0),
         axis=1,
         keepdims=True,
     )
-    own_basis = basis_ref[...].astype(jnp.float32)
+    fetch_basis.wait()
+    own_basis = basis_vmem[...].astype(jnp.float32)
     own_wide = jnp.concatenate(
         [own_basis, jnp.broadcast_to(density_col, (rows, LANES - width))], axis=1
     )
@@ -166,7 +175,7 @@
             jax.ShapeDtypeStruct((rows, width), jnp.bfloat16),
             jax.ShapeDtypeStruct((width, width), jnp.float32),
         ),
-        in_specs=[pl.BlockSpec(memory_space=pl.ANY), vmem, vmem],
+        in_specs=[pl.BlockSpec(memory_space=pltpu.HBM)] * 3,
         out_specs=(vmem, vmem),
         scratch_shapes=[
             pltpu.VMEM((n, rows, features // n), jnp.bfloat16),
@@ -174,12 +183,14 @@
             pltpu.VMEM((n, rows, total), jnp.float32),
             pltpu.VMEM((n, rows, total), jnp.float32),
             pltpu.VMEM((n, rows, LANES), jnp.float32),
-            pltpu.SemaphoreType.DMA,
+            pltpu.VMEM((rows, width), jnp.bfloat16),
+            pltpu.VMEM((1, rows), jnp.bfloat16),
+            pltpu.SemaphoreType.DMA((3,)),
             pltpu.SemaphoreType.DMA((4,)),
             pltpu.SemaphoreType.DMA((4,)),
         ],
         compiler_params=pltpu.CompilerParams(
-            collective_id=0, has_side_effects=True, vmem_limit_bytes=32 * 1024 * 1024
+            collective_id=0, has_side_effects=True, vmem_limit_bytes=64 * 1024 * 1024
         ),
         cost_estimate=pl.CostEstimate(
             flops=2 * total * total * (features // n),

time: 27.3 us -> 27.5 us (level)
  Pallas kernels: 23 us -> 24 us
  local copies, waits for them, and re-layouts: 3.47 us -> 2.6 us
    pallas_call x1, Pallas kernels: 23 us -> 24 us  [shards(): pl.pallas_call(functools.partial(kernel, n), out_shape=(jax.ShapeDtypeStr...]
    unnamed x8 -> x4, local copies, waits for them, and re-layouts: 3.47 us -> 2.6 us
where the time goes in v2:
time: 27.5 us; the launch traced here: 27.2 us
  Pallas kernels  24 us (87%)
  local copies, waits for them, and re-layouts  2.6 us (9%)
  between operations  0.65 us (2%)
    pallas_call x1, Pallas kernels, shards(): pl.pallas_call(functools.partial(kernel, n), out_shape=(jax.ShapeDtypeStr...  24 us
    unnamed x4, local copies, waits for them, and re-layouts  2.6 us

profile of v2, /device:TPU:0, one launch (start us, length us, event | category | flops | bytes accessed | tf_op | source)
XLA Modules:
  0.0 27.2 jit_solution(935310891804493891)
XLA Ops:
  0.6 24.0 %shard_map.50 = (bf16[8,64]{1,0:T(8,128)(2,1)}, f32[64,64]{1,0:T(8,128)}) custom-call(bf16[8,16384]{1,0:T(8,128)(2,1)} %frames_ref.1, bf16[8,64]{1,0:T(8,128)(2,1)} %basis_ref.1, bf16[1,8]{1,0:T(2,128)(2,1)} %bitcast.1), custom_call_target="tpu_custom_call" | custom-call | flops 33554432 | bytes 262144 | tf_op jit(solution)/shard_map/pallas_call | solution.py:172
  24.6 0.0 copy-start
  24.6 0.6 %copy-done = bf16[8,64]{1,0:T(8,128)(2,1)S(1)} copy-done((bf16[8,64]{1,0:T(8,128)(2,1)S(1)}, bf16[8,64]{1,0:T(8,128)(2,1)}, u32[]{:S(2)}) %copy-start) | copy-done | bytes 1048
  25.3 0.6 %copy.7 = bf16[8,64]{1,0:T(8,128)(2,1)} copy(bf16[8,64]{1,0:T(8,128)(2,1)S(1)} %copy-done) | data formatting | bytes 2048
  25.9 1.4 %copy.8 = f32[64,64]{1,0:T(8,128)} copy(f32[64,64]{1,0:T(8,128)} %get-tuple-element.5) | data formatting | bytes 32768
Async XLA Ops:
  24.6 0.7 %copy-start = (bf16[8,64]{1,0:T(8,128)(2,1)S(1)}, bf16[8,64]{1,0:T(8,128)(2,1)}, u32[]{:S(2)}) copy-start(bf16[8,64]{1,0:T(8,128)(2,1)} %get-tuple-element.4) | copy-start | bytes 3076

commit v3 on v2

--- a/solution.py
+++ b/solution.py
@@ -12,10 +12,13 @@
 
 def partners(me, n):
     half = n // 2
-    mine = me // half
-    far = [(1 - mine) * half + lax.rem(me + j, half) for j in range(half)]
-    near = [mine * half + lax.rem(me + j, half) for j in range(1, half)]
-    return far + near
+    upper = me >= half
+    place = jnp.where(upper, me - half, me)
+    mine = jnp.where(upper, half, 0)
+    turned = [place] + [
+        jnp.where(place >= half - j, place + j - half, place + j) for j in range(1, half)
+    ]
+    return [half - mine + t for t in turned] + [mine + t for t in turned[1:]]
 
 
 def kernel(
@@ -23,8 +26,7 @@
     frames_ref,
     basis_ref,
     density_ref,
-    residual_ref,
-    coef_ref,
+    both_ref,
     gathered,
     aux,
     partial,
@@ -107,18 +109,18 @@
         jnp.int32, (total, total), 1
     )
     density_all = jnp.sum(jnp.where(eye, wide[:, width : width + 1], 0.0), axis=0, keepdims=True)
-    lane = lax.broadcasted_iota(jnp.int32, (total, LANES), 1)
-    vectors = jnp.where(lane < width, wide, 0.0)
-    vectors_bf = vectors.astype(jnp.bfloat16)
-    own_lane = lax.broadcasted_iota(jnp.int32, (rows, LANES), 1)
-    own_vectors = jnp.where(own_lane < width, own_wide, 0.0)
+    vectors = wide[:, :width]
+    twice = jnp.concatenate([vectors, vectors], axis=1).astype(jnp.bfloat16)
     overlap = lax.dot_general(
-        own_vectors.astype(jnp.bfloat16),
-        vectors_bf,
+        own_basis.astype(jnp.bfloat16),
+        vectors.astype(jnp.bfloat16),
         (((1,), (1,)), ((), ())),
         preferred_element_type=jnp.float32,
     )
-    onto = jnp.concatenate([jnp.transpose(vectors)[:width], overlap], axis=0)
+    overlap_high = overlap.astype(jnp.bfloat16).astype(jnp.float32)
+    onto = jnp.concatenate(
+        [jnp.transpose(wide)[:width], overlap_high, overlap - overlap_high], axis=0
+    ).astype(jnp.bfloat16)
 
     own.wait()
     wait_all(gathered, recv_sem.at[0])
@@ -140,28 +142,33 @@
 
     squared_dist = jnp.sum(arrived[...], axis=0)
     weight = (jnp.exp(-squared_dist / features) * density_all).astype(jnp.bfloat16)
-    numer = jnp.dot(weight, vectors_bf, preferred_element_type=jnp.float32)
+    numer = jnp.dot(weight, twice, preferred_element_type=jnp.float32)
     totals = jnp.sum(weight.astype(jnp.float32), axis=1, keepdims=True)
     own_applied = numer / totals
-    applied[me] = own_applied
+    high = own_applied.astype(jnp.bfloat16).astype(jnp.float32)
+    lane = lax.broadcasted_iota(jnp.int32, (rows, LANES), 1)
+    applied[me] = jnp.where(lane < width, high, own_applied - high).astype(jnp.bfloat16)
     for other in others:
         send(applied.at[me], applied.at[me], 3, other)
     wait_all(applied, recv_sem.at[3])
 
     products = jnp.dot(
-        onto,
-        applied[...].reshape(total, LANES),
-        precision=lax.Precision.HIGHEST,
-        preferred_element_type=jnp.float32,
-    )
-    coef_ref[...] = products[:width, :width]
-    residual = own_applied - products[width:] / total
-    residual_ref[...] = residual[:, :width].astype(jnp.bfloat16)
+        onto, applied[...].reshape(total, LANES), preferred_element_type=jnp.float32
+    )
+    products = products[:, :width] + products[:, width : 2 * width]
+    both_ref[:width] = products[:width]
+    projection = products[width : width + rows] + products[width + rows :]
+    both_ref[width:] = own_applied[:, :width] - projection / total
 
     wait_all(gathered, send_sem.at[0])
     wait_all(aux, send_sem.at[1])
     wait_all(arrived, send_sem.at[2])
     wait_all(applied, send_sem.at[3])
+
+
+def finish(width, both_ref, residual_ref, coef_ref):
+    coef_ref[...] = both_ref[:width]
+    residual_ref[...] = both_ref[width:].astype(jnp.bfloat16)
 
 
 def shards(n, frames, basis, density):
@@ -169,20 +176,18 @@
     width = basis.shape[1]
     total = n * rows
     vmem = pl.BlockSpec(memory_space=pltpu.VMEM)
-    return pl.pallas_call(
+    operands = (frames, basis, density.reshape(1, rows))
+    both = pl.pallas_call(
         functools.partial(kernel, n),
-        out_shape=(
-            jax.ShapeDtypeStruct((rows, width), jnp.bfloat16),
-            jax.ShapeDtypeStruct((width, width), jnp.float32),
-        ),
+        out_shape=jax.ShapeDtypeStruct((width + rows, width), jnp.float32),
         in_specs=[pl.BlockSpec(memory_space=pltpu.HBM)] * 3,
-        out_specs=(vmem, vmem),
+        out_specs=vmem,
         scratch_shapes=[
             pltpu.VMEM((n, rows, features // n), jnp.bfloat16),
             pltpu.VMEM((n, rows, LANES), jnp.bfloat16),
             pltpu.VMEM((n, rows, total), jnp.float32),
             pltpu.VMEM((n, rows, total), jnp.float32),
-            pltpu.VMEM((n, rows, LANES), jnp.float32),
+            pltpu.VMEM((n, rows, LANES), jnp.bfloat16),
             pltpu.VMEM((rows, width), jnp.bfloat16),
             pltpu.VMEM((1, rows), jnp.bfloat16),
             pltpu.SemaphoreType.DMA((3,)),
@@ -190,14 +195,23 @@
             pltpu.SemaphoreType.DMA((4,)),
         ],
         compiler_params=pltpu.CompilerParams(
-            collective_id=0, has_side_effects=True, vmem_limit_bytes=64 * 1024 * 1024
+            collective_id=0, has_side_effects=True, vmem_limit_bytes=32 * 1024 * 1024
         ),
         cost_estimate=pl.CostEstimate(
             flops=2 * total * total * (features // n),
             bytes_accessed=2 * rows * features,
             transcendentals=rows * total,
         ),
-    )(frames, basis, density.reshape(1, rows))
+    )(*(pltpu.with_memory_space_constraint(x, pltpu.HBM) for x in operands))
+    return pl.pallas_call(
+        functools.partial(finish, width),
+        out_shape=(
+            jax.ShapeDtypeStruct((rows, width), jnp.bfloat16),
+            jax.ShapeDtypeStruct((width, width), jnp.float32),
+        ),
+        in_specs=[vmem],
+        out_specs=(vmem, vmem),
+    )(both)
 
 
 def solution(mesh):

time: 27.5 us -> 26.1 us (0.949)
  local copies, waits for them, and re-layouts: 2.6 us -> 0.61 us
  Pallas kernels: 24 us -> 24.7 us
    unnamed x4 -> x2, local copies, waits for them, and re-layouts: 2.6 us -> 0.61 us
    pallas_call x1 -> x2, Pallas kernels: 24 us -> 24.7 us  [the longest x1 23.3 us: shards(): pl.pallas_call(functools.partial(kernel, n), out_shape=jax.ShapeDtypeStru...]
where the time goes in v3:
time: 26.1 us; the launch traced here: 25.9 us
  Pallas kernels  24.7 us (95%)
  between operations  0.65 us (2%)
  local copies, waits for them, and re-layouts  0.61 us (2%)
    pallas_call x1, Pallas kernels, shards(): pl.pallas_call(functools.partial(kernel, n), out_shape=jax.ShapeDtypeStru...  23.3 us
    pallas_call x1, Pallas kernels, shards(): pl.pallas_call(functools.partial(finish, width), out_shape=(jax.ShapeDtyp...  1.38 us
    unnamed x2, local copies, waits for them, and re-layouts  0.61 us

profile of v3, /device:TPU:0, one launch (start us, length us, event | category | flops | bytes accessed | tf_op | source)
XLA Modules:
  0.0 25.9 jit_solution(17852493949546960753)
XLA Ops:
  0.6 23.3 %shard_map.50.both_ref = f32[72,64]{1,0:T(8,128)S(1)} custom-call(bf16[8,16384]{1,0:T(8,128)(2,1)} %frames_ref.1, bf16[8,64]{1,0:T(8,128)(2,1)} %basis_ref.1, bf16[1,8]{1,0:T(2,128)(2,1)} %bitcast.1), custom_call_target="tpu_custom_call" | custom-call | flops 33554432 | bytes 262144 | tf_op jit(solution)/shard_map/pallas_call | solution.py:180
  23.9 0.0 copy-start
  23.9 0.6 %copy-done = f32[72,64]{1,0:T(8,128)} copy-done((f32[72,64]{1,0:T(8,128)}, f32[72,64]{1,0:T(8,128)S(1)}, u32[]{:S(2)}) %copy-start) | copy-done | bytes 18456
  24.5 1.4 %shard_map.51 = (bf16[8,64]{1,0:T(8,128)(2,1)}, f32[64,64]{1,0:T(8,128)}) custom-call(f32[72,64]{1,0:T(8,128)} %copy-done), custom_call_target="tpu_custom_call" | custom-call | tf_op jit(solution)/shard_map/pallas_call | solution.py:206
Async XLA Ops:
  23.9 0.6 %copy-start = (f32[72,64]{1,0:T(8,128)}, f32[72,64]{1,0:T(8,128)S(1)}, u32[]{:S(2)}) copy-start(f32[72,64]{1,0:T(8,128)S(1)} %shard_map.50.both_ref) | copy-start | bytes 55300

commit v4 on v3

--- a/solution.py
+++ b/solution.py
@@ -26,7 +26,8 @@
     frames_ref,
     basis_ref,
     density_ref,
-    both_ref,
+    residual_ref,
+    coef_ref,
     gathered,
     aux,
     partial,
@@ -134,13 +135,13 @@
         + jnp.sum(diagonal, axis=0, keepdims=True)
         - 2.0 * gram
     )
-    partial[...] = dist.reshape(n, rows, total)
+    partial[...] = dist.reshape(n, rows, total).astype(jnp.bfloat16)
     for other in others:
         send(partial.at[other], arrived.at[me], 2, other)
     arrived[me] = partial[me]
     wait_all(arrived, recv_sem.at[2])
 
-    squared_dist = jnp.sum(arrived[...], axis=0)
+    squared_dist = jnp.sum(arrived[...].astype(jnp.float32), axis=0)
     weight = (jnp.exp(-squared_dist / features) * density_all).astype(jnp.bfloat16)
     numer = jnp.dot(weight, twice, preferred_element_type=jnp.float32)
     totals = jnp.sum(weight.astype(jnp.float32), axis=1, keepdims=True)
@@ -156,19 +157,14 @@
         onto, applied[...].reshape(total, LANES), preferred_element_type=jnp.float32
     )
     products = products[:, :width] + products[:, width : 2 * width]
-    both_ref[:width] = products[:width]
+    coef_ref[...] = products[:width]
     projection = products[width : width + rows] + products[width + rows :]
-    both_ref[width:] = own_applied[:, :width] - projection / total
+    residual_ref[...] = (own_applied[:, :width] - projection / total).astype(jnp.bfloat16)
 
     wait_all(gathered, send_sem.at[0])
     wait_all(aux, send_sem.at[1])
     wait_all(arrived, send_sem.at[2])
     wait_all(applied, send_sem.at[3])
-
-
-def finish(width, both_ref, residual_ref, coef_ref):
-    coef_ref[...] = both_ref[:width]
-    residual_ref[...] = both_ref[width:].astype(jnp.bfloat16)
 
 
 def shards(n, frames, basis, density):
@@ -177,16 +173,19 @@
     total = n * rows
     vmem = pl.BlockSpec(memory_space=pltpu.VMEM)
     operands = (frames, basis, density.reshape(1, rows))
-    both = pl.pallas_call(
+    return pl.pallas_call(
         functools.partial(kernel, n),
-        out_shape=jax.ShapeDtypeStruct((width + rows, width), jnp.float32),
+        out_shape=(
+            jax.ShapeDtypeStruct((rows, width), jnp.bfloat16),
+            jax.ShapeDtypeStruct((width, width), jnp.float32),
+        ),
         in_specs=[pl.BlockSpec(memory_space=pltpu.HBM)] * 3,
-        out_specs=vmem,
+        out_specs=(vmem, vmem),
         scratch_shapes=[
             pltpu.VMEM((n, rows, features // n), jnp.bfloat16),
             pltpu.VMEM((n, rows, LANES), jnp.bfloat16),
-            pltpu.VMEM((n, rows, total), jnp.float32),
-            pltpu.VMEM((n, rows, total), jnp.float32),
+            pltpu.VMEM((n, rows, total), jnp.bfloat16),
+            pltpu.VMEM((n, rows, total), jnp.bfloat16),
             pltpu.VMEM((n, rows, LANES), jnp.bfloat16),
             pltpu.VMEM((rows, width), jnp.bfloat16),
             pltpu.VMEM((1, rows), jnp.bfloat16),
@@ -203,15 +202,6 @@
             transcendentals=rows * total,
         ),
     )(*(pltpu.with_memory_space_constraint(x, pltpu.HBM) for x in operands))
-    return pl.pallas_call(
-        functools.partial(finish, width),
-        out_shape=(
-            jax.ShapeDtypeStruct((rows, width), jnp.bfloat16),
-            jax.ShapeDtypeStruct((width, width), jnp.float32),
-        ),
-        in_specs=[vmem],
-        out_specs=(vmem, vmem),
-    )(both)
 
 
 def solution(mesh):

time: 26.1 us -> 25.1 us (0.962)
  Pallas kernels: 24.7 us -> 23.1 us
  local copies, waits for them, and re-layouts: 0.61 us -> 1.19 us
    pallas_call x2 -> x1, Pallas kernels: 24.7 us -> 23.1 us  [shards(): pl.pallas_call(functools.partial(kernel, n), out_shape=(jax.ShapeDtypeStr...]
    unnamed x2, local copies, waits for them, and re-layouts: 0.61 us -> 1.19 us
where the time goes in v4:
time: 25.1 us; the launch traced here: 24.9 us
  Pallas kernels  23.1 us (92%)
  local copies, waits for them, and re-layouts  1.19 us (5%)
  between operations  0.64 us (3%)
    pallas_call x1, Pallas kernels, shards(): pl.pallas_call(functools.partial(kernel, n), out_shape=(jax.ShapeDtypeStr...  23.1 us
    unnamed x2, local copies, waits for them, and re-layouts  1.19 us

profile of v4, /device:TPU:0, one launch (start us, length us, event | category | flops | bytes accessed | tf_op | source)
XLA Modules:
  0.0 24.9 jit_solution(3489414400188412231)
XLA Ops:
  0.6 23.1 %shard_map.50 = (bf16[8,64]{1,0:T(8,128)(2,1)S(1)}, f32[64,64]{1,0:T(8,128)S(1)}) custom-call(bf16[8,16384]{1,0:T(8,128)(2,1)} %frames_ref.1, bf16[8,64]{1,0:T(8,128)(2,1)} %basis_ref.1, bf16[1,8]{1,0:T(2,128)(2,1)} %bitcast.1), custom_call_target="tpu_custom_call" | custom-call | flops 33554432 | bytes 262144 | tf_op jit(solution)/shard_map/pallas_call | solution.py:176
  23.8 0.6 %copy.7 = bf16[8,64]{1,0:T(8,128)(2,1)} copy(bf16[8,64]{1,0:T(8,128)(2,1)S(1)} %get-tuple-element.4) | data formatting | bytes 2048
  24.3 0.6 %copy.8 = f32[64,64]{1,0:T(8,128)} copy(f32[64,64]{1,0:T(8,128)S(1)} %get-tuple-element.5) | data formatting | bytes 32768

commit v5 on v4

--- a/solution.py
+++ b/solution.py
@@ -35,6 +35,7 @@
     applied,
     basis_vmem,
     density_vmem,
+    staged,
     own_sem,
     send_sem,
     recv_sem,
@@ -46,6 +47,8 @@
     total = n * rows
     others = partners(me, n)
 
+    stage = pltpu.make_async_copy(frames_ref, staged, own_sem.at[0])
+    stage.start()
     fetch_basis = pltpu.make_async_copy(basis_ref, basis_vmem, own_sem.at[1])
     fetch_basis.start()
     fetch_density = pltpu.make_async_copy(density_ref, density_vmem, own_sem.at[2])
@@ -56,27 +59,6 @@
         pl.semaphore_signal(
             barrier, inc=1, device_id={"blk": other}, device_id_type=pl.DeviceIdType.MESH
         )
-
-    own = pltpu.make_async_copy(
-        frames_ref.at[:, pl.ds(pl.multiple_of(me * span, span), span)], gathered.at[me], own_sem.at[0]
-    )
-    own.start()
-
-    row_id = lax.broadcasted_iota(jnp.int32, (rows, rows), 0)
-    col_id = lax.broadcasted_iota(jnp.int32, (rows, rows), 1)
-    fetch_density.wait()
-    density_row = density_vmem[...].astype(jnp.float32)
-    density_col = jnp.sum(
-        jnp.where(row_id == col_id, jnp.broadcast_to(density_row, (rows, rows)), 0.0),
-        axis=1,
-        keepdims=True,
-    )
-    fetch_basis.wait()
-    own_basis = basis_vmem[...].astype(jnp.float32)
-    own_wide = jnp.concatenate(
-        [own_basis, jnp.broadcast_to(density_col, (rows, LANES - width))], axis=1
-    )
-    aux[me] = own_wide.astype(jnp.bfloat16)
 
     pl.semaphore_wait(barrier, n - 1)
 
@@ -94,35 +76,40 @@
         part = buffer.at[pl.ds(0, n - 1)]
         pltpu.make_async_copy(part, part, sem).wait()
 
+    stage.wait()
     for other in others:
         send(
-            frames_ref.at[:, pl.ds(pl.multiple_of(other * span, span), span)],
+            staged.at[:, pl.ds(pl.multiple_of(other * span, span), span)],
             gathered.at[me],
             0,
             other,
         )
+    own = pltpu.make_async_copy(
+        staged.at[:, pl.ds(pl.multiple_of(me * span, span), span)], gathered.at[me], own_sem.at[3]
+    )
+    own.start()
+
+    row_id = lax.broadcasted_iota(jnp.int32, (rows, rows), 0)
+    col_id = lax.broadcasted_iota(jnp.int32, (rows, rows), 1)
+    fetch_density.wait()
+    density_row = density_vmem[...].astype(jnp.float32)
+    density_col = jnp.sum(
+        jnp.where(row_id == col_id, jnp.broadcast_to(density_row, (rows, rows)), 0.0),
+        axis=1,
+        keepdims=True,
+    )
+    fetch_basis.wait()
+    own_basis = basis_vmem[...].astype(jnp.float32)
+    own_wide = jnp.concatenate(
+        [own_basis, jnp.broadcast_to(density_col, (rows, LANES - width))], axis=1
+    )
+    aux[me] = own_wide.astype(jnp.bfloat16)
     for other in others:
         send(aux.at[me], aux.at[me], 1, other)
 
-    wait_all(aux, recv_sem.at[1])
-    wide = aux[...].astype(jnp.float32).reshape(total, LANES)
     eye = lax.broadcasted_iota(jnp.int32, (total, total), 0) == lax.broadcasted_iota(
         jnp.int32, (total, total), 1
     )
-    density_all = jnp.sum(jnp.where(eye, wide[:, width : width + 1], 0.0), axis=0, keepdims=True)
-    vectors = wide[:, :width]
-    twice = jnp.concatenate([vectors, vectors], axis=1).astype(jnp.bfloat16)
-    overlap = lax.dot_general(
-        own_basis.astype(jnp.bfloat16),
-        vectors.astype(jnp.bfloat16),
-        (((1,), (1,)), ((), ())),
-        preferred_element_type=jnp.float32,
-    )
-    overlap_high = overlap.astype(jnp.bfloat16).astype(jnp.float32)
-    onto = jnp.concatenate(
-        [jnp.transpose(wide)[:width], overlap_high, overlap - overlap_high], axis=0
-    ).astype(jnp.bfloat16)
-
     own.wait()
     wait_all(gathered, recv_sem.at[0])
     block = gathered[...].reshape(total, span)
@@ -139,6 +126,13 @@
     for other in others:
         send(partial.at[other], arrived.at[me], 2, other)
     arrived[me] = partial[me]
+
+    wait_all(aux, recv_sem.at[1])
+    wide = aux[...].astype(jnp.float32).reshape(total, LANES)
+    density_all = jnp.sum(jnp.where(eye, wide[:, width : width + 1], 0.0), axis=0, keepdims=True)
+    vectors = wide[:, :width]
+    twice = jnp.concatenate([vectors, vectors], axis=1).astype(jnp.bfloat16)
+
     wait_all(arrived, recv_sem.at[2])
 
     squared_dist = jnp.sum(arrived[...].astype(jnp.float32), axis=0)
@@ -151,6 +145,18 @@
     applied[me] = jnp.where(lane < width, high, own_applied - high).astype(jnp.bfloat16)
     for other in others:
         send(applied.at[me], applied.at[me], 3, other)
+
+    overlap = lax.dot_general(
+        own_basis.astype(jnp.bfloat16),
+        vectors.astype(jnp.bfloat16),
+        (((1,), (1,)), ((), ())),
+        preferred_element_type=jnp.float32,
+    )
+    overlap_high = overlap.astype(jnp.bfloat16).astype(jnp.float32)
+    onto = jnp.concatenate(
+        [jnp.transpose(wide)[:width], overlap_high, overlap - overlap_high], axis=0
+    ).astype(jnp.bfloat16)
+
     wait_all(applied, recv_sem.at[3])
 
     products = jnp.dot(
@@ -189,7 +195,8 @@
             pltpu.VMEM((n, rows, LANES), jnp.bfloat16),
             pltpu.VMEM((rows, width), jnp.bfloat16),
             pltpu.VMEM((1, rows), jnp.bfloat16),
-            pltpu.SemaphoreType.DMA((3,)),
+            pltpu.VMEM((rows, features), jnp.bfloat16),
+            pltpu.SemaphoreType.DMA((4,)),
             pltpu.SemaphoreType.DMA((4,)),
             pltpu.SemaphoreType.DMA((4,)),
         ],

time: 25.1 us -> 24.3 us (0.968)
  Pallas kernels: 23.1 us -> 22.4 us
    pallas_call x1, Pallas kernels: 23.1 us -> 22.4 us  [shards(): pl.pallas_call(functools.partial(kernel, n), out_shape=(jax.ShapeDtypeStr...]
where the time goes in v5:
time: 24.3 us; the launch traced here: 24.2 us
  Pallas kernels  22.4 us (92%)
  local copies, waits for them, and re-layouts  1.19 us (5%)
  between operations  0.64 us (3%)
    pallas_call x1, Pallas kernels, shards(): pl.pallas_call(functools.partial(kernel, n), out_shape=(jax.ShapeDtypeStr...  22.4 us
    unnamed x2, local copies, waits for them, and re-layouts  1.19 us

profile of v5, /device:TPU:0, one launch (start us, length us, event | category | flops | bytes accessed | tf_op | source)
XLA Modules:
  0.0 24.2 jit_solution(4067331459333753446)
XLA Ops:
  0.6 22.4 %shard_map.50 = (bf16[8,64]{1,0:T(8,128)(2,1)S(1)}, f32[64,64]{1,0:T(8,128)S(1)}) custom-call(bf16[8,16384]{1,0:T(8,128)(2,1)} %frames_ref.1, bf16[8,64]{1,0:T(8,128)(2,1)} %basis_ref.1, bf16[1,8]{1,0:T(2,128)(2,1)} %bitcast.1), custom_call_target="tpu_custom_call" | custom-call | flops 33554432 | bytes 262144 | tf_op jit(solution)/shard_map/pallas_call | solution.py:182
  23.0 0.6 %copy.7 = bf16[8,64]{1,0:T(8,128)(2,1)} copy(bf16[8,64]{1,0:T(8,128)(2,1)S(1)} %get-tuple-element.4) | data formatting | bytes 2048
  23.6 0.6 %copy.8 = f32[64,64]{1,0:T(8,128)} copy(f32[64,64]{1,0:T(8,128)S(1)} %get-tuple-element.5) | data formatting | bytes 32768

commit v6 on v5

--- a/solution.py
+++ b/solution.py
@@ -8,6 +8,7 @@
 from jax.sharding import PartitionSpec as P
 
 LANES = 128
+CHUNKS = 2
 
 
 def partners(me, n):
@@ -44,6 +45,7 @@
     rows, features = frames_ref.shape
     width = basis_ref.shape[1]
     span = features // n
+    piece = span // CHUNKS
     total = n * rows
     others = partners(me, n)
 
@@ -77,17 +79,19 @@
         pltpu.make_async_copy(part, part, sem).wait()
 
     stage.wait()
-    for other in others:
-        send(
-            staged.at[:, pl.ds(pl.multiple_of(other * span, span), span)],
-            gathered.at[me],
-            0,
-            other,
+    def columns(owner, chunk):
+        return staged.at[:, pl.ds(pl.multiple_of(owner * span + chunk * piece, piece), piece)]
+
+    own = []
+    for chunk in range(CHUNKS):
+        for other in others:
+            send(columns(other, chunk), gathered.at[chunk, me], 3 + chunk, other)
+        own.append(
+            pltpu.make_async_copy(
+                columns(me, chunk), gathered.at[chunk, me], own_sem.at[3 + chunk]
+            )
         )
-    own = pltpu.make_async_copy(
-        staged.at[:, pl.ds(pl.multiple_of(me * span, span), span)], gathered.at[me], own_sem.at[3]
-    )
-    own.start()
+        own[chunk].start()
 
     row_id = lax.broadcasted_iota(jnp.int32, (rows, rows), 0)
     col_id = lax.broadcasted_iota(jnp.int32, (rows, rows), 1)
@@ -105,17 +109,19 @@
     )
     aux[me] = own_wide.astype(jnp.bfloat16)
     for other in others:
-        send(aux.at[me], aux.at[me], 1, other)
+        send(aux.at[me], aux.at[me], 0, other)
 
     eye = lax.broadcasted_iota(jnp.int32, (total, total), 0) == lax.broadcasted_iota(
         jnp.int32, (total, total), 1
     )
-    own.wait()
-    wait_all(gathered, recv_sem.at[0])
-    block = gathered[...].reshape(total, span)
-    gram = lax.dot_general(
-        block, block, (((1,), (1,)), ((), ())), preferred_element_type=jnp.float32
-    )
+    gram = jnp.zeros((total, total), jnp.float32)
+    for chunk in range(CHUNKS):
+        own[chunk].wait()
+        wait_all(gathered.at[chunk], recv_sem.at[3 + chunk])
+        block = gathered[chunk].reshape(total, piece)
+        gram += lax.dot_general(
+            block, block, (((1,), (1,)), ((), ())), preferred_element_type=jnp.float32
+        )
     diagonal = jnp.where(eye, gram, 0.0)
     dist = (
         jnp.sum(diagonal, axis=1, keepdims=True)
@@ -124,16 +130,16 @@
     )
     partial[...] = dist.reshape(n, rows, total).astype(jnp.bfloat16)
     for other in others:
-        send(partial.at[other], arrived.at[me], 2, other)
+        send(partial.at[other], arrived.at[me], 1, other)
     arrived[me] = partial[me]
 
-    wait_all(aux, recv_sem.at[1])
+    wait_all(aux, recv_sem.at[0])
     wide = aux[...].astype(jnp.float32).reshape(total, LANES)
     density_all = jnp.sum(jnp.where(eye, wide[:, width : width + 1], 0.0), axis=0, keepdims=True)
     vectors = wide[:, :width]
     twice = jnp.concatenate([vectors, vectors], axis=1).astype(jnp.bfloat16)
 
-    wait_all(arrived, recv_sem.at[2])
+    wait_all(arrived, recv_sem.at[1])
 
     squared_dist = jnp.sum(arrived[...].astype(jnp.float32), axis=0)
     weight = (jnp.exp(-squared_dist / features) * density_all).astype(jnp.bfloat16)
@@ -144,7 +150,7 @@
     lane = lax.broadcasted_iota(jnp.int32, (rows, LANES), 1)
     applied[me] = jnp.where(lane < width, high, own_applied - high).astype(jnp.bfloat16)
     for other in others:
-        send(applied.at[me], applied.at[me], 3, other)
+        send(applied.at[me], applied.at[me], 2, other)
 
     overlap = lax.dot_general(
         own_basis.astype(jnp.bfloat16),
@@ -157,7 +163,7 @@
         [jnp.transpose(wide)[:width], overlap_high, overlap - overlap_high], axis=0
     ).astype(jnp.bfloat16)
 
-    wait_all(applied, recv_sem.at[3])
+    wait_all(applied, recv_sem.at[2])
 
     products = jnp.dot(
         onto, applied[...].reshape(total, LANES), preferred_element_type=jnp.float32
@@ -167,10 +173,11 @@
     projection = products[width : width + rows] + products[width + rows :]
     residual_ref[...] = (own_applied[:, :width] - projection / total).astype(jnp.bfloat16)
 
-    wait_all(gathered, send_sem.at[0])
-    wait_all(aux, send_sem.at[1])
-    wait_all(arrived, send_sem.at[2])
-    wait_all(applied, send_sem.at[3])
+    wait_all(aux, send_sem.at[0])
+    wait_all(arrived, send_sem.at[1])
+    wait_all(applied, send_sem.at[2])
+    for chunk in range(CHUNKS):
+        wait_all(gathered.at[chunk], send_sem.at[3 + chunk])
 
 
 def shards(n, frames, basis, density):
@@ -188,7 +195,7 @@
         in_specs=[pl.BlockSpec(memory_space=pltpu.HBM)] * 3,
         out_specs=(vmem, vmem),
         scratch_shapes=[
-            pltpu.VMEM((n, rows, features // n), jnp.bfloat16),
+            pltpu.VMEM((CHUNKS, n, rows, features // n // CHUNKS), jnp.bfloat16),
             pltpu.VMEM((n, rows, LANES), jnp.bfloat16),
             pltpu.VMEM((n, rows, total), jnp.bfloat16),
             pltpu.VMEM((n, rows, total), jnp.bfloat16),
@@ -196,9 +203,9 @@
             pltpu.VMEM((rows, width), jnp.bfloat16),
             pltpu.VMEM((1, rows), jnp.bfloat16),
             pltpu.VMEM((rows, features), jnp.bfloat16),
-            pltpu.SemaphoreType.DMA((4,)),
-            pltpu.SemaphoreType.DMA((4,)),
-            pltpu.SemaphoreType.DMA((4,)),
+            pltpu.SemaphoreType.DMA((3 + CHUNKS,)),
+            pltpu.SemaphoreType.DMA((3 + CHUNKS,)),
+            pltpu.SemaphoreType.DMA((3 + CHUNKS,)),
         ],
         compiler_params=pltpu.CompilerParams(
             collective_id=0, has_side_effects=True, vmem_limit_bytes=32 * 1024 * 1024

time: 24.3 us -> 24.4 us (level)
  no operation moved by 1% of the time
where the time goes in v6:
time: 24.4 us; the launch traced here: 24.2 us
  Pallas kernels  22.4 us (92%)
  local copies, waits for them, and re-layouts  1.19 us (5%)
  between operations  0.64 us (3%)
    pallas_call x1, Pallas kernels, shards(): pl.pallas_call(functools.partial(kernel, n), out_shape=(jax.ShapeDtypeStr...  22.4 us
    unnamed x2, local copies, waits for them, and re-layouts  1.19 us

profile of v6, /device:TPU:0, one launch (start us, length us, event | category | flops | bytes accessed | tf_op | source)
XLA Modules:
  0.0 24.2 jit_solution(1913354913683781872)
XLA Ops:
  0.6 22.4 %shard_map.50 = (bf16[8,64]{1,0:T(8,128)(2,1)S(1)}, f32[64,64]{1,0:T(8,128)S(1)}) custom-call(bf16[8,16384]{1,0:T(8,128)(2,1)} %frames_ref.1, bf16[8,64]{1,0:T(8,128)(2,1)} %basis_ref.1, bf16[1,8]{1,0:T(2,128)(2,1)} %bitcast.1), custom_call_target="tpu_custom_call" | custom-call | flops 33554432 | bytes 262144 | tf_op jit(solution)/shard_map/pallas_call | solution.py:189
  23.0 0.6 %copy.7 = bf16[8,64]{1,0:T(8,128)(2,1)} copy(bf16[8,64]{1,0:T(8,128)(2,1)S(1)} %get-tuple-element.4) | data formatting | bytes 2048
  23.6 0.6 %copy.8 = f32[64,64]{1,0:T(8,128)} copy(f32[64,64]{1,0:T(8,128)S(1)} %get-tuple-element.5) | data formatting | bytes 32768

commit v7 on v5

--- a/solution.py
+++ b/solution.py
@@ -10,15 +10,18 @@
 LANES = 128
 
 
-def partners(me, n):
+def for_partners(me, n, body):
     half = n // 2
     upper = me >= half
     place = jnp.where(upper, me - half, me)
     mine = jnp.where(upper, half, 0)
-    turned = [place] + [
-        jnp.where(place >= half - j, place + j - half, place + j) for j in range(1, half)
-    ]
-    return [half - mine + t for t in turned] + [mine + t for t in turned[1:]]
+
+    @pl.loop(0, n - 1)
+    def _(k):
+        far = k < half
+        turned = place + jnp.where(far, k, k - half + 1)
+        turned = jnp.where(turned >= half, turned - half, turned)
+        body(turned + jnp.where(far, half - mine, mine))
 
 
 def kernel(
@@ -45,7 +48,6 @@
     width = basis_ref.shape[1]
     span = features // n
     total = n * rows
-    others = partners(me, n)
 
     stage = pltpu.make_async_copy(frames_ref, staged, own_sem.at[0])
     stage.start()
@@ -55,11 +57,12 @@
     fetch_density.start()
 
     barrier = pltpu.get_barrier_semaphore()
-    for other in others:
+    def greet(other):
         pl.semaphore_signal(
             barrier, inc=1, device_id={"blk": other}, device_id_type=pl.DeviceIdType.MESH
         )
 
+    for_partners(me, n, greet)
     pl.semaphore_wait(barrier, n - 1)
 
     def send(src, dst, slot, other):
@@ -77,16 +80,12 @@
         pltpu.make_async_copy(part, part, sem).wait()
 
     stage.wait()
-    for other in others:
-        send(
-            staged.at[:, pl.ds(pl.multiple_of(other * span, span), span)],
-            gathered.at[me],
-            0,
-            other,
-        )
-    own = pltpu.make_async_copy(
-        staged.at[:, pl.ds(pl.multiple_of(me * span, span), span)], gathered.at[me], own_sem.at[3]
-    )
+
+    def columns(owner):
+        return staged.at[:, pl.ds(pl.multiple_of(owner * span, span), span)]
+
+    for_partners(me, n, lambda other: send(columns(other), gathered.at[me], 0, other))
+    own = pltpu.make_async_copy(columns(me), gathered.at[me], own_sem.at[3])
     own.start()
 
     row_id = lax.broadcasted_iota(jnp.int32, (rows, rows), 0)
@@ -104,8 +103,7 @@
         [own_basis, jnp.broadcast_to(density_col, (rows, LANES - width))], axis=1
     )
     aux[me] = own_wide.astype(jnp.bfloat16)
-    for other in others:
-        send(aux.at[me], aux.at[me], 1, other)
+    for_partners(me, n, lambda other: send(aux.at[me], aux.at[me], 1, other))
 
     eye = lax.broadcasted_iota(jnp.int32, (total, total), 0) == lax.broadcasted_iota(
         jnp.int32, (total, total), 1
@@ -123,8 +121,7 @@
         - 2.0 * gram
     )
     partial[...] = dist.reshape(n, rows, total).astype(jnp.bfloat16)
-    for other in others:
-        send(partial.at[other], arrived.at[me], 2, other)
+    for_partners(me, n, lambda other: send(partial.at[other], arrived.at[me], 2, other))
     arrived[me] = partial[me]
 
     wait_all(aux, recv_sem.at[1])
@@ -143,8 +140,7 @@
     high = own_applied.astype(jnp.bfloat16).astype(jnp.float32)
     lane = lax.broadcasted_iota(jnp.int32, (rows, LANES), 1)
     applied[me] = jnp.where(lane < width, high, own_applied - high).astype(jnp.bfloat16)
-    for other in others:
-        send(applied.at[me], applied.at[me], 3, other)
+    for_partners(me, n, lambda other: send(applied.at[me], applied.at[me], 3, other))
 
     overlap = lax.dot_general(
         own_basis.astype(jnp.bfloat16),

time: 24.3 us -> 24.4 us (level)
  no operation moved by 1% of the time
where the time goes in v7:
time: 24.4 us; the launch traced here: 24.2 us
  Pallas kernels  22.4 us (92%)
  local copies, waits for them, and re-layouts  1.19 us (5%)
  between operations  0.64 us (3%)
    pallas_call x1, Pallas kernels, shards(): pl.pallas_call(functools.partial(kernel, n), out_shape=(jax.ShapeDtypeStr...  22.4 us
    unnamed x2, local copies, waits for them, and re-layouts  1.19 us

profile of v7, /device:TPU:0, one launch (start us, length us, event | category | flops | bytes accessed | tf_op | source)
XLA Modules:
  0.0 24.2 jit_solution(984392566275458244)
XLA Ops:
  0.6 22.4 %shard_map.50 = (bf16[8,64]{1,0:T(8,128)(2,1)S(1)}, f32[64,64]{1,0:T(8,128)S(1)}) custom-call(bf16[8,16384]{1,0:T(8,128)(2,1)} %frames_ref.1, bf16[8,64]{1,0:T(8,128)(2,1)} %basis_ref.1, bf16[1,8]{1,0:T(2,128)(2,1)} %bitcast.1), custom_call_target="tpu_custom_call" | custom-call | flops 33554432 | bytes 262144 | tf_op jit(solution)/shard_map/pallas_call | solution.py:178
  23.1 0.6 %copy.7 = bf16[8,64]{1,0:T(8,128)(2,1)} copy(bf16[8,64]{1,0:T(8,128)(2,1)S(1)} %get-tuple-element.4) | data formatting | bytes 2048
  23.6 0.6 %copy.8 = f32[64,64]{1,0:T(8,128)} copy(f32[64,64]{1,0:T(8,128)S(1)} %get-tuple-element.5) | data formatting | bytes 32768

commit v8 on v5

--- a/solution.py
+++ b/solution.py
@@ -19,6 +19,12 @@
         jnp.where(place >= half - j, place + j - half, place + j) for j in range(1, half)
     ]
     return [half - mine + t for t in turned] + [mine + t for t in turned[1:]]
+
+
+def alternate(others):
+    half = (len(others) + 1) // 2
+    far, near = others[:half], others[half:]
+    return [pick for pair in zip(far, near) for pick in pair] + [far[-1]]
 
 
 def kernel(
@@ -47,18 +53,18 @@
     total = n * rows
     others = partners(me, n)
 
+    barrier = pltpu.get_barrier_semaphore()
+    for other in others:
+        pl.semaphore_signal(
+            barrier, inc=1, device_id={"blk": other}, device_id_type=pl.DeviceIdType.MESH
+        )
+
     stage = pltpu.make_async_copy(frames_ref, staged, own_sem.at[0])
     stage.start()
     fetch_basis = pltpu.make_async_copy(basis_ref, basis_vmem, own_sem.at[1])
     fetch_basis.start()
     fetch_density = pltpu.make_async_copy(density_ref, density_vmem, own_sem.at[2])
     fetch_density.start()
-
-    barrier = pltpu.get_barrier_semaphore()
-    for other in others:
-        pl.semaphore_signal(
-            barrier, inc=1, device_id={"blk": other}, device_id_type=pl.DeviceIdType.MESH
-        )
 
     pl.semaphore_wait(barrier, n - 1)
 
@@ -77,7 +83,7 @@
         pltpu.make_async_copy(part, part, sem).wait()
 
     stage.wait()
-    for other in others:
+    for other in alternate(others):
         send(
             staged.at[:, pl.ds(pl.multiple_of(other * span, span), span)],
             gathered.at[me],

time: 24.3 us -> 24.4 us (level)
  no operation moved by 1% of the time
where the time goes in v8:
time: 24.4 us; the launch traced here: 24.3 us
  Pallas kernels  22.4 us (92%)
  local copies, waits for them, and re-layouts  1.19 us (5%)
  between operations  0.64 us (3%)
    pallas_call x1, Pallas kernels, shards(): pl.pallas_call(functools.partial(kernel, n), out_shape=(jax.ShapeDtypeStr...  22.4 us
    unnamed x2, local copies, waits for them, and re-layouts  1.19 us

profile of v8, /device:TPU:0, one launch (start us, length us, event | category | flops | bytes accessed | tf_op | source)
XLA Modules:
  0.0 24.3 jit_solution(9929331397701423797)
XLA Ops:
  0.6 22.4 %shard_map.50 = (bf16[8,64]{1,0:T(8,128)(2,1)S(1)}, f32[64,64]{1,0:T(8,128)S(1)}) custom-call(bf16[8,16384]{1,0:T(8,128)(2,1)} %frames_ref.1, bf16[8,64]{1,0:T(8,128)(2,1)} %basis_ref.1, bf16[1,8]{1,0:T(2,128)(2,1)} %bitcast.1), custom_call_target="tpu_custom_call" | custom-call | flops 33554432 | bytes 262144 | tf_op jit(solution)/shard_map/pallas_call | solution.py:188
  23.1 0.6 %copy.7 = bf16[8,64]{1,0:T(8,128)(2,1)} copy(bf16[8,64]{1,0:T(8,128)(2,1)S(1)} %get-tuple-element.4) | data formatting | bytes 2048
  23.6 0.6 %copy.8 = f32[64,64]{1,0:T(8,128)} copy(f32[64,64]{1,0:T(8,128)S(1)} %get-tuple-element.5) | data formatting | bytes 32768

commit v9 on v8

--- a/solution.py
+++ b/solution.py
@@ -19,6 +19,22 @@
         jnp.where(place >= half - j, place + j - half, place + j) for j in range(1, half)
     ]
     return [half - mine + t for t in turned] + [mine + t for t in turned[1:]]
+
+
+def farthest_first(me, n):
+    fours = n // 4
+    four, place = me // 4, lax.rem(me, 4)
+    turned = [jnp.where(place >= 4 - j, place + j - 4, place + j) for j in range(4)]
+    upper = 2 * four >= fours
+    beyond = jnp.where(upper, four, fours - 1 - four)
+    order = []
+    for k in range(fours - 1):
+        outer = k < beyond
+        ahead = jnp.where(outer, fours - 1 - k, k - beyond)
+        behind = jnp.where(outer, k, fours - 1 - k + beyond)
+        first = 4 * jnp.where(upper, behind, ahead)
+        order += [first + t for t in turned]
+    return order + [4 * four + t for t in turned[1:]]
 
 
 def alternate(others):
@@ -52,9 +68,10 @@
     span = features // n
     total = n * rows
     others = partners(me, n)
+    by_distance = farthest_first(me, n)
 
     barrier = pltpu.get_barrier_semaphore()
-    for other in others:
+    for other in by_distance:
         pl.semaphore_signal(
             barrier, inc=1, device_id={"blk": other}, device_id_type=pl.DeviceIdType.MESH
         )
@@ -95,6 +112,14 @@
     )
     own.start()
 
+    own_frames = staged[...].astype(jnp.float32)
+    own_norms = jnp.sum(own_frames * own_frames, axis=1, keepdims=True)
+    norm_parts = []
+    rest = own_norms
+    for _ in range(3):
+        norm_parts.append(rest.astype(jnp.bfloat16).astype(jnp.float32))
+        rest = rest - norm_parts[-1]
+
     row_id = lax.broadcasted_iota(jnp.int32, (rows, rows), 0)
     col_id = lax.broadcasted_iota(jnp.int32, (rows, rows), 1)
     fetch_density.wait()
@@ -106,11 +131,14 @@
     )
     fetch_basis.wait()
     own_basis = basis_vmem[...].astype(jnp.float32)
+    lane = lax.broadcasted_iota(jnp.int32, (rows, LANES), 1)
     own_wide = jnp.concatenate(
         [own_basis, jnp.broadcast_to(density_col, (rows, LANES - width))], axis=1
     )
+    for index, part in enumerate(norm_parts):
+        own_wide = jnp.where(lane == width + 1 + index, part, own_wide)
     aux[me] = own_wide.astype(jnp.bfloat16)
-    for other in others:
+    for other in by_distance:
         send(aux.at[me], aux.at[me], 1, other)
 
     eye = lax.broadcasted_iota(jnp.int32, (total, total), 0) == lax.broadcasted_iota(
@@ -122,34 +150,29 @@
     gram = lax.dot_general(
         block, block, (((1,), (1,)), ((), ())), preferred_element_type=jnp.float32
     )
-    diagonal = jnp.where(eye, gram, 0.0)
-    dist = (
-        jnp.sum(diagonal, axis=1, keepdims=True)
-        + jnp.sum(diagonal, axis=0, keepdims=True)
-        - 2.0 * gram
-    )
-    partial[...] = dist.reshape(n, rows, total).astype(jnp.bfloat16)
-    for other in others:
+    partial[...] = gram.reshape(n, rows, total)
+    for other in by_distance:
         send(partial.at[other], arrived.at[me], 2, other)
     arrived[me] = partial[me]
 
     wait_all(aux, recv_sem.at[1])
     wide = aux[...].astype(jnp.float32).reshape(total, LANES)
     density_all = jnp.sum(jnp.where(eye, wide[:, width : width + 1], 0.0), axis=0, keepdims=True)
+    norms = sum(wide[:, width + 1 + index : width + 2 + index] for index in range(3))
+    norm_sums = own_norms + jnp.sum(jnp.where(eye, norms, 0.0), axis=0, keepdims=True)
     vectors = wide[:, :width]
     twice = jnp.concatenate([vectors, vectors], axis=1).astype(jnp.bfloat16)
 
     wait_all(arrived, recv_sem.at[2])
 
-    squared_dist = jnp.sum(arrived[...].astype(jnp.float32), axis=0)
-    weight = (jnp.exp(-squared_dist / features) * density_all).astype(jnp.bfloat16)
+    squared_dist = norm_sums - 2.0 * jnp.sum(arrived[...], axis=0)
+    weight = (jnp.exp(squared_dist * (-1.0 / features)) * density_all).astype(jnp.bfloat16)
     numer = jnp.dot(weight, twice, preferred_element_type=jnp.float32)
     totals = jnp.sum(weight.astype(jnp.float32), axis=1, keepdims=True)
     own_applied = numer / totals
     high = own_applied.astype(jnp.bfloat16).astype(jnp.float32)
-    lane = lax.broadcasted_iota(jnp.int32, (rows, LANES), 1)
     applied[me] = jnp.where(lane < width, high, own_applied - high).astype(jnp.bfloat16)
-    for other in others:
+    for other in by_distance:
         send(applied.at[me], applied.at[me], 3, other)
 
     overlap = lax.dot_general(
@@ -171,7 +194,7 @@
     products = products[:, :width] + products[:, width : 2 * width]
     coef_ref[...] = products[:width]
     projection = products[width : width + rows] + products[width + rows :]
-    residual_ref[...] = (own_applied[:, :width] - projection / total).astype(jnp.bfloat16)
+    residual_ref[...] = (own_applied[:, :width] - projection * (1.0 / total)).astype(jnp.bfloat16)
 
     wait_all(gathered, send_sem.at[0])
     wait_all(aux, send_sem.at[1])
@@ -196,8 +219,8 @@
         scratch_shapes=[
             pltpu.VMEM((n, rows, features // n), jnp.bfloat16),
             pltpu.VMEM((n, rows, LANES), jnp.bfloat16),
-            pltpu.VMEM((n, rows, total), jnp.bfloat16),
-            pltpu.VMEM((n, rows, total), jnp.bfloat16),
+            pltpu.VMEM((n, rows, total), jnp.float32),
+            pltpu.VMEM((n, rows, total), jnp.float32),
             pltpu.VMEM((n, rows, LANES), jnp.bfloat16),
             pltpu.VMEM((rows, width), jnp.bfloat16),
             pltpu.VMEM((1, rows), jnp.bfloat16),

time: 24.4 us -> 24.3 us (level)
  no operation moved by 1% of the time
where the time goes in v9:
time: 24.3 us; the launch traced here: 24.2 us
  Pallas kernels  22.4 us (92%)
  local copies, waits for them, and re-layouts  1.19 us (5%)
  between operations  0.64 us (3%)
    pallas_call x1, Pallas kernels, shards(): pl.pallas_call(functools.partial(kernel, n), out_shape=(jax.ShapeDtypeStr...  22.4 us
    unnamed x2, local copies, waits for them, and re-layouts  1.19 us

profile of v9, /device:TPU:0, one launch (start us, length us, event | category | flops | bytes accessed | tf_op | source)
XLA Modules:
  0.0 24.2 jit_solution(13846688686128315122)
XLA Ops:
  0.6 22.4 %shard_map.50 = (bf16[8,64]{1,0:T(8,128)(2,1)S(1)}, f32[64,64]{1,0:T(8,128)S(1)}) custom-call(bf16[8,16384]{1,0:T(8,128)(2,1)} %frames_ref.1, bf16[8,64]{1,0:T(8,128)(2,1)} %basis_ref.1, bf16[1,8]{1,0:T(2,128)(2,1)} %bitcast.1), custom_call_target="tpu_custom_call" | custom-call | flops 33554432 | bytes 262144 | tf_op jit(solution)/shard_map/pallas_call | solution.py:211
  23.0 0.6 %copy.7 = bf16[8,64]{1,0:T(8,128)(2,1)} copy(bf16[8,64]{1,0:T(8,128)(2,1)S(1)} %get-tuple-element.4) | data formatting | bytes 2048
  23.6 0.6 %copy.8 = f32[64,64]{1,0:T(8,128)} copy(f32[64,64]{1,0:T(8,128)S(1)} %get-tuple-element.5) | data formatting | bytes 32768

commit v10 on v9

--- a/solution.py
+++ b/solution.py
@@ -202,18 +202,30 @@
     wait_all(applied, send_sem.at[3])
 
 
+def deliver(residual_vmem, coef_vmem, residual_ref, coef_ref, sem):
+    copies = [
+        pltpu.make_async_copy(coef_vmem, coef_ref, sem.at[0]),
+        pltpu.make_async_copy(residual_vmem, residual_ref, sem.at[1]),
+    ]
+    for copy in copies:
+        copy.start()
+    for copy in copies:
+        copy.wait()
+
+
 def shards(n, frames, basis, density):
     rows, features = frames.shape
     width = basis.shape[1]
     total = n * rows
     vmem = pl.BlockSpec(memory_space=pltpu.VMEM)
     operands = (frames, basis, density.reshape(1, rows))
-    return pl.pallas_call(
+    out_shape = (
+        jax.ShapeDtypeStruct((rows, width), jnp.bfloat16),
+        jax.ShapeDtypeStruct((width, width), jnp.float32),
+    )
+    results = pl.pallas_call(
         functools.partial(kernel, n),
-        out_shape=(
-            jax.ShapeDtypeStruct((rows, width), jnp.bfloat16),
-            jax.ShapeDtypeStruct((width, width), jnp.float32),
-        ),
+        out_shape=out_shape,
         in_specs=[pl.BlockSpec(memory_space=pltpu.HBM)] * 3,
         out_specs=(vmem, vmem),
         scratch_shapes=[
@@ -238,6 +250,14 @@
             transcendentals=rows * total,
         ),
     )(*(pltpu.with_memory_space_constraint(x, pltpu.HBM) for x in operands))
+    return pl.pallas_call(
+        deliver,
+        out_shape=out_shape,
+        in_specs=[vmem, vmem],
+        out_specs=(pl.BlockSpec(memory_space=pltpu.HBM),) * 2,
+        scratch_shapes=[pltpu.SemaphoreType.DMA((2,))],
+        compiler_params=pltpu.CompilerParams(vmem_limit_bytes=1024 * 1024),
+    )(*(pltpu.with_memory_space_constraint(x, pltpu.VMEM) for x in results))
 
 
 def solution(mesh):

time: 24.3 us -> 23.8 us (0.979)
  local copies, waits for them, and re-layouts: 1.19 us -> 0 us
  Pallas kernels: 22.4 us -> 23 us
    unnamed x2 -> x0, local copies, waits for them, and re-layouts: 1.19 us -> none
    pallas_call x1 -> x2, Pallas kernels: 22.4 us -> 23 us  [the longest x1 22.4 us: shards(): pl.pallas_call(functools.partial(kernel, n), out_shape=out_shape, in_spec...]
where the time goes in v10:
time: 23.8 us; the launch traced here: 23.6 us
  Pallas kernels  23 us (97%)
  between operations  0.64 us (3%)
    pallas_call x1, Pallas kernels, shards(): pl.pallas_call(functools.partial(kernel, n), out_shape=out_shape, in_spec...  22.4 us
    pallas_call x1, Pallas kernels, shards(): pl.pallas_call(deliver, out_shape=out_shape, in_specs=[vmem, vmem], out_s...  0.64 us

profile of v10, /device:TPU:0, one launch (start us, length us, event | category | flops | bytes accessed | tf_op | source)
XLA Modules:
  0.0 23.6 jit_solution(18081190618968123069)
XLA Ops:
  0.6 22.4 %shard_map.50 = (bf16[8,64]{1,0:T(8,128)(2,1)S(1)}, f32[64,64]{1,0:T(8,128)S(1)}) custom-call(bf16[8,16384]{1,0:T(8,128)(2,1)} %frames_ref.1, bf16[8,64]{1,0:T(8,128)(2,1)} %basis_ref.1, bf16[1,8]{1,0:T(2,128)(2,1)} %bitcast.1), custom_call_target="tpu_custom_call" | custom-call | flops 33554432 | bytes 262144 | tf_op jit(solution)/shard_map/pallas_call | solution.py:226
  23.0 0.6 %shard_map.51 = (bf16[8,64]{1,0:T(8,128)(2,1)}, f32[64,64]{1,0:T(8,128)}) custom-call(bf16[8,64]{1,0:T(8,128)(2,1)S(1)} %get-tuple-element.4.residual_vmem, f32[64,64]{1,0:T(8,128)S(1)} %get-tuple-element.5.coef_vmem), custom_call_target="tpu_custom_call" | custom-call | tf_op jit(solution)/shard_map/pallas_call | solution.py:253

commit v11 on v10

--- a/solution.py
+++ b/solution.py
@@ -8,17 +8,6 @@
 from jax.sharding import PartitionSpec as P
 
 LANES = 128
-
-
-def partners(me, n):
-    half = n // 2
-    upper = me >= half
-    place = jnp.where(upper, me - half, me)
-    mine = jnp.where(upper, half, 0)
-    turned = [place] + [
-        jnp.where(place >= half - j, place + j - half, place + j) for j in range(1, half)
-    ]
-    return [half - mine + t for t in turned] + [mine + t for t in turned[1:]]
 
 
 def farthest_first(me, n):
@@ -35,12 +24,6 @@
         first = 4 * jnp.where(upper, behind, ahead)
         order += [first + t for t in turned]
     return order + [4 * four + t for t in turned[1:]]
-
-
-def alternate(others):
-    half = (len(others) + 1) // 2
-    far, near = others[:half], others[half:]
-    return [pick for pair in zip(far, near) for pick in pair] + [far[-1]]
 
 
 def kernel(
@@ -67,11 +50,10 @@
     width = basis_ref.shape[1]
     span = features // n
     total = n * rows
-    others = partners(me, n)
-    by_distance = farthest_first(me, n)
+    others = farthest_first(me, n)
 
     barrier = pltpu.get_barrier_semaphore()
-    for other in by_distance:
+    for other in others:
         pl.semaphore_signal(
             barrier, inc=1, device_id={"blk": other}, device_id_type=pl.DeviceIdType.MESH
         )
@@ -100,7 +82,7 @@
         pltpu.make_async_copy(part, part, sem).wait()
 
     stage.wait()
-    for other in alternate(others):
+    for other in others:
         send(
             staged.at[:, pl.ds(pl.multiple_of(other * span, span), span)],
             gathered.at[me],
@@ -138,7 +120,7 @@
     for index, part in enumerate(norm_parts):
         own_wide = jnp.where(lane == width + 1 + index, part, own_wide)
     aux[me] = own_wide.astype(jnp.bfloat16)
-    for other in by_distance:
+    for other in others:
         send(aux.at[me], aux.at[me], 1, other)
 
     eye = lax.broadcasted_iota(jnp.int32, (total, total), 0) == lax.broadcasted_iota(
@@ -151,7 +133,7 @@
         block, block, (((1,), (1,)), ((), ())), preferred_element_type=jnp.float32
     )
     partial[...] = gram.reshape(n, rows, total)
-    for other in by_distance:
+    for other in others:
         send(partial.at[other], arrived.at[me], 2, other)
     arrived[me] = partial[me]
 
@@ -172,7 +154,7 @@
     own_applied = numer / totals
     high = own_applied.astype(jnp.bfloat16).astype(jnp.float32)
     applied[me] = jnp.where(lane < width, high, own_applied - high).astype(jnp.bfloat16)
-    for other in by_distance:
+    for other in others:
         send(applied.at[me], applied.at[me], 3, other)
 
     overlap = lax.dot_general(

time: 23.8 us -> 23.1 us (0.971)
  Pallas kernels: 23 us -> 22.3 us
    pallas_call x1, Pallas kernels: 22.4 us -> 21.7 us  [shards(): pl.pallas_call(functools.partial(kernel, n), out_shape=out_shape, in_spec...]
where the time goes in v11:
time: 23.1 us; the launch traced here: 22.9 us
  Pallas kernels  22.3 us (97%)
  between operations  0.64 us (3%)
    pallas_call x1, Pallas kernels, shards(): pl.pallas_call(functools.partial(kernel, n), out_shape=out_shape, in_spec...  21.7 us
    pallas_call x1, Pallas kernels, shards(): pl.pallas_call(deliver, out_shape=out_shape, in_specs=[vmem, vmem], out_s...  0.64 us

profile of v11, /device:TPU:0, one launch (start us, length us, event | category | flops | bytes accessed | tf_op | source)
XLA Modules:
  0.0 22.9 jit_solution(3475268650561370014)
XLA Ops:
  0.6 21.7 %shard_map.50 = (bf16[8,64]{1,0:T(8,128)(2,1)S(1)}, f32[64,64]{1,0:T(8,128)S(1)}) custom-call(bf16[8,16384]{1,0:T(8,128)(2,1)} %frames_ref.1, bf16[8,64]{1,0:T(8,128)(2,1)} %basis_ref.1, bf16[1,8]{1,0:T(2,128)(2,1)} %bitcast.1), custom_call_target="tpu_custom_call" | custom-call | flops 33554432 | bytes 262144 | tf_op jit(solution)/shard_map/pallas_call | solution.py:208
  22.3 0.6 %shard_map.51 = (bf16[8,64]{1,0:T(8,128)(2,1)}, f32[64,64]{1,0:T(8,128)}) custom-call(bf16[8,64]{1,0:T(8,128)(2,1)S(1)} %get-tuple-element.4.residual_vmem, f32[64,64]{1,0:T(8,128)S(1)} %get-tuple-element.5.coef_vmem), custom_call_target="tpu_custom_call" | custom-call | tf_op jit(solution)/shard_map/pallas_call | solution.py:235

commit v12 on v11

--- a/solution.py
+++ b/solution.py
@@ -120,6 +120,7 @@
     for index, part in enumerate(norm_parts):
         own_wide = jnp.where(lane == width + 1 + index, part, own_wide)
     aux[me] = own_wide.astype(jnp.bfloat16)
+    wait_all(gathered, send_sem.at[0])
     for other in others:
         send(aux.at[me], aux.at[me], 1, other)
 
@@ -168,6 +169,8 @@
         [jnp.transpose(wide)[:width], overlap_high, overlap - overlap_high], axis=0
     ).astype(jnp.bfloat16)
 
+    wait_all(aux, send_sem.at[1])
+    wait_all(arrived, send_sem.at[2])
     wait_all(applied, recv_sem.at[3])
 
     products = jnp.dot(
@@ -178,9 +181,6 @@
     projection = products[width : width + rows] + products[width + rows :]
     residual_ref[...] = (own_applied[:, :width] - projection * (1.0 / total)).astype(jnp.bfloat16)
 
-    wait_all(gathered, send_sem.at[0])
-    wait_all(aux, send_sem.at[1])
-    wait_all(arrived, send_sem.at[2])
     wait_all(applied, send_sem.at[3])
 
 

time: 23.1 us -> 22.8 us (0.987)
    pallas_call x1, Pallas kernels: 21.7 us -> 21.4 us  [shards(): pl.pallas_call(functools.partial(kernel, n), out_shape=out_shape, in_spec...]
where the time goes in v12:
time: 22.8 us; the launch traced here: 22.7 us
  Pallas kernels  22.1 us (97%)
  between operations  0.64 us (3%)
    pallas_call x1, Pallas kernels, shards(): pl.pallas_call(functools.partial(kernel, n), out_shape=out_shape, in_spec...  21.4 us
    pallas_call x1, Pallas kernels, shards(): pl.pallas_call(deliver, out_shape=out_shape, in_specs=[vmem, vmem], out_s...  0.64 us

profile of v12, /device:TPU:0, one launch (start us, length us, event | category | flops | bytes accessed | tf_op | source)
XLA Modules:
  0.0 22.7 jit_solution(16521564134636820813)
XLA Ops:
  0.6 21.4 %shard_map.50 = (bf16[8,64]{1,0:T(8,128)(2,1)S(1)}, f32[64,64]{1,0:T(8,128)S(1)}) custom-call(bf16[8,16384]{1,0:T(8,128)(2,1)} %frames_ref.1, bf16[8,64]{1,0:T(8,128)(2,1)} %basis_ref.1, bf16[1,8]{1,0:T(2,128)(2,1)} %bitcast.1), custom_call_target="tpu_custom_call" | custom-call | flops 33554432 | bytes 262144 | tf_op jit(solution)/shard_map/pallas_call | solution.py:208
  22.1 0.6 %shard_map.51 = (bf16[8,64]{1,0:T(8,128)(2,1)}, f32[64,64]{1,0:T(8,128)}) custom-call(bf16[8,64]{1,0:T(8,128)(2,1)S(1)} %get-tuple-element.4.residual_vmem, f32[64,64]{1,0:T(8,128)S(1)} %get-tuple-element.5.coef_vmem), custom_call_target="tpu_custom_call" | custom-call | tf_op jit(solution)/shard_map/pallas_call | solution.py:235

commit v13 on v12

--- a/solution.py
+++ b/solution.py
@@ -81,10 +81,11 @@
         part = buffer.at[pl.ds(0, n - 1)]
         pltpu.make_async_copy(part, part, sem).wait()
 
-    stage.wait()
-    for other in others:
+    for index, other in enumerate(others):
+        if index == 4:
+            stage.wait()
         send(
-            staged.at[:, pl.ds(pl.multiple_of(other * span, span), span)],
+            (frames_ref if index < 4 else staged).at[:, pl.ds(pl.multiple_of(other * span, span), span)],
             gathered.at[me],
             0,
             other,

time: 22.8 us -> 23 us (level)
  no operation moved by 1% of the time
where the time goes in v13:
time: 23 us; the launch traced here: 22.9 us
  Pallas kernels  22.3 us (97%)
  between operations  0.64 us (3%)
    pallas_call x1, Pallas kernels, shards(): pl.pallas_call(functools.partial(kernel, n), out_shape=out_shape, in_spec...  21.6 us
    pallas_call x1, Pallas kernels, shards(): pl.pallas_call(deliver, out_shape=out_shape, in_specs=[vmem, vmem], out_s...  0.64 us

profile of v13, /device:TPU:0, one launch (start us, length us, event | category | flops | bytes accessed | tf_op | source)
XLA Modules:
  0.0 22.9 jit_solution(2553834711108779816)
XLA Ops:
  0.6 21.6 %shard_map.50 = (bf16[8,64]{1,0:T(8,128)(2,1)S(1)}, f32[64,64]{1,0:T(8,128)S(1)}) custom-call(bf16[8,16384]{1,0:T(8,128)(2,1)} %frames_ref.1, bf16[8,64]{1,0:T(8,128)(2,1)} %basis_ref.1, bf16[1,8]{1,0:T(2,128)(2,1)} %bitcast.1), custom_call_target="tpu_custom_call" | custom-call | flops 33554432 | bytes 262144 | tf_op jit(solution)/shard_map/pallas_call | solution.py:209
  22.3 0.6 %shard_map.51 = (bf16[8,64]{1,0:T(8,128)(2,1)}, f32[64,64]{1,0:T(8,128)}) custom-call(bf16[8,64]{1,0:T(8,128)(2,1)S(1)} %get-tuple-element.4.residual_vmem, f32[64,64]{1,0:T(8,128)S(1)} %get-tuple-element.5.coef_vmem), custom_call_target="tpu_custom_call" | custom-call | tf_op jit(solution)/shard_map/pallas_call | solution.py:236
